TPU v7x, 32 devices: a whole 2x2x4 slice. The times are simulated.
32 devices in a mesh: parts: 1, sec: 32 (over z, y, x, core).
Axes of the slice: x: 2, y: 2, z: 4, core: 2. Of those that a mesh axis runs over, the one named last changes fastest.
Arguments:
- queries: bfloat16 [8192, 1024], P(('parts', 'sec')), may hold values from -6 to 6
- keys: bfloat16 [8192, 1024], P(('parts', 'sec')), may hold values from -6 to 6
- values: bfloat16 [8192, 2048], P(('parts', 'sec')), may hold values from -6 to 6
- gate_codes: int32 [8192, 16], P(('parts', 'sec')), may hold values from 0 to 5734
- beta_codes: int32 [8192, 16], P(('parts', 'sec')), may hold values from 16 to 4096
- norm_gain: float32 [128], replicated, may hold values from 0.5 to 1.5
Outputs:
- head_out: bfloat16 [8192, 2048], P(('parts', 'sec'))
- final_state: float32 [2048, 128], P(('parts', 'sec'))
All inputs are finite; a program needn't handle non-finite values.
Results may differ from a plain program's by a relative error of at most 0.001.
Values sent between devices are 32-bit elements; how exact they have to be, the bound alone decides.
A program may use at most 320 MiB of HBM per device.

v0:
```python
import jax
import jax.numpy as jnp
from jax import lax
from jax.sharding import PartitionSpec as P

DK = 128
SPAN = 64


def entering(part, axis, combine, identity):
    place = lax.axis_index(axis)
    gathered = jax.tree.map(lambda a: lax.all_gather(a, axis), part)
    state = jax.tree.map(lambda a, e: jnp.zeros_like(a) + jnp.asarray(e, a.dtype), part, identity)

    def one(hop, state):
        return combine(
            state, jax.tree.map(lambda a: lax.dynamic_index_in_dim(a, hop, 0, False), gathered)
        )

    return lax.fori_loop(0, place, one, state)


def broadcast(value, axis, source):
    kept = jnp.where(lax.axis_index(axis) == source, value, 0).astype(value.dtype)
    return lax.psum(kept, axis)


def normalize(rows, factor):
    return rows * lax.rsqrt(jnp.sum(rows * rows, axis=-1, keepdims=True) + 1e-06) * factor


def matrix_product(form, left, right):
    return jnp.einsum(form, left, right, precision=lax.Precision.HIGHEST)


def compose(earlier, later):
    first_map, first_state = earlier
    second_map, second_state = later
    return (
        matrix_product("hij,hjk->hik", second_map, first_map),
        matrix_product("hij,hjv->hiv", second_map, first_state) + second_state,
    )


def block_step(carried, block_in):
    transition_matrix, state_matrix = carried
    query_rows, key_matrix, value_rows, log_decay, beta_rows = block_in
    length = query_rows.shape[1]
    key_width = key_matrix.shape[2]
    decay_factor = jnp.exp(jnp.cumsum(log_decay, axis=1))
    row_index = lax.broadcasted_iota(jnp.int32, (length, length), 0)
    col_ids = lax.broadcasted_iota(jnp.int32, (length, length), 1)
    strict_mask = (row_index > col_ids).astype(jnp.float32)
    lower_mask = (row_index >= col_ids).astype(jnp.float32)
    identity_c = jnp.eye(length, dtype=jnp.float32)
    inner_kk = matrix_product("hik,hjk->hij", key_matrix, key_matrix)
    coupling = beta_rows[:, :, None] * inner_kk * strict_mask
    inverse = identity_c - coupling
    power_mat = coupling
    for doubling in range(1, length.bit_length() - 1):
        power_mat = matrix_product("hij,hjk->hik", power_mat, power_mat)
        inverse = matrix_product("hij,hjk->hik", inverse, identity_c + power_mat)
    right_side = jnp.concatenate(
        [
            beta_rows[:, :, None] * key_matrix,
            beta_rows[:, :, None] * value_rows / decay_factor[:, :, None],
        ],
        axis=-1,
    )
    solved = matrix_product("hij,hjk->hik", inverse, right_side)
    erase_rows = solved[:, :, :key_width]
    written_rows = solved[:, :, key_width:]
    scores = matrix_product("hik,hjk->hij", query_rows, key_matrix) * lower_mask
    projected_value = decay_factor[:, :, None] * (
        query_rows - matrix_product("hij,hjk->hik", scores, erase_rows)
    )
    section_output = matrix_product("wjf,wft->wjt", projected_value, state_matrix) + decay_factor[
        :, :, None
    ] * matrix_product("hij,hjv->hiv", scores, written_rows)
    carried_transform = matrix_product("hik,hkm->him", projected_value, transition_matrix)
    final_decay = decay_factor[:, -1][:, None, None]
    erase_key = matrix_product("hjk,hjm->hkm", key_matrix, erase_rows)
    write_key = matrix_product("ius,iuc->isc", key_matrix, written_rows)
    transition_matrix = final_decay * (
        transition_matrix - matrix_product("hkm,hmn->hkn", erase_key, transition_matrix)
    )
    state_matrix = final_decay * (
        state_matrix - matrix_product("cjg,cgu->cju", erase_key, state_matrix) + write_key
    )
    return ((transition_matrix, state_matrix), (section_output, carried_transform))


def shards(queries, keys, values, gate_codes, beta_codes, norm_gain):
    tokens_dev, heads = gate_codes.shape
    width = norm_gain.shape[0]
    key_width = DK
    group = heads // (queries.shape[1] // key_width)
    sections = lax.axis_size("sec")
    total = tokens_dev * sections
    query_rows = normalize(
        queries.astype(jnp.float32).reshape(tokens_dev, -1, key_width), key_width ** (-0.5)
    )
    key_matrix = normalize(keys.astype(jnp.float32).reshape(tokens_dev, -1, key_width), 1.0)
    query_rows = jnp.repeat(query_rows, group, axis=1)
    key_matrix = jnp.repeat(key_matrix, group, axis=1)
    value_rows = values.astype(jnp.float32).reshape(tokens_dev, heads, width)
    log_decay = -gate_codes.astype(jnp.float32) / total
    beta_rows = beta_codes.astype(jnp.float32) / total
    count = tokens_dev // SPAN

    def blocked(array):
        shaped = array.reshape((count, SPAN) + array.shape[1:])
        return jnp.swapaxes(shaped, 1, 2)

    inputs = (
        blocked(query_rows),
        blocked(key_matrix),
        blocked(value_rows),
        blocked(log_decay),
        blocked(beta_rows),
    )
    identity_k = jnp.broadcast_to(
        jnp.eye(key_width, dtype=jnp.float32), (heads, key_width, key_width)
    )
    zero_state = jnp.zeros((heads, key_width, width), jnp.float32)
    (transition_matrix, state_matrix), (section_output, carried_transform) = lax.scan(
        block_step, (identity_k, zero_state), inputs
    )
    section_output = jnp.swapaxes(section_output, 0, 1).reshape(heads, tokens_dev, width)
    carried_transform = jnp.swapaxes(carried_transform, 0, 1).reshape(heads, tokens_dev, key_width)
    entering_state = entering(
        (transition_matrix, state_matrix), "sec", compose, (identity_k, zero_state)
    )[1]
    output_rows = section_output + matrix_product("wjf,wft->wjt", carried_transform, entering_state)
    scaled = (
        output_rows
        * lax.rsqrt(jnp.mean(output_rows * output_rows, axis=-1, keepdims=True) + 1e-06)
        * norm_gain
    )
    head_out = jnp.swapaxes(scaled, 0, 1).reshape(tokens_dev, heads * width).astype(jnp.bfloat16)
    ending_state = (
        matrix_product("cjg,cgu->cju", transition_matrix, entering_state) + state_matrix
    ).reshape(heads * key_width, width)
    row_count = heads * key_width // sections
    whole = broadcast(ending_state, "sec", sections - 1)
    final_state = lax.dynamic_slice_in_dim(whole, lax.axis_index("sec") * row_count, row_count, 0)
    return (head_out, final_state)


def solution(mesh):
    in_specs = (
        P(("parts", "sec"), None),
        P(("parts", "sec"), None),
        P(("parts", "sec"), None),
        P(("parts", "sec"), None),
        P(("parts", "sec"), None),
        P(),
    )
    out_specs = (P(("parts", "sec"), None), P(("parts", "sec"), None))
    return jax.shard_map(shards, mesh=mesh, in_specs=in_specs, out_specs=out_specs, check_vma=False)
```

profile of v0, /device:TPU:29, one launch (start us, length us, event | category | flops | bytes accessed | tf_op | source)
XLA Modules:
  0.0 773.9 jit_solution(4461835839426412052)
XLA Ops:
  18.6 139.3 %while.30 = (s32[]{:T(128)}, f32[16,128,128]{2,1,0:T(8,128)}, f32[16,128,128]{2,1,0:T(8,128)}, f32[4,16,64,128]{3,2,0,1:T(8,128)}, f32[4,16,64,128]{3,2,0,1:T(8,...) while((s32[]{:T(128)}, f32[16,128,128]{2,1,0:T(8,128)}, ...), condition=%wide.region_4.5_spmd.clone, body=%wide.region_2.4_spmd.clone.sunk | while | flops 2721602560 | bytes 44791276 | solution.py:126
  38.4 2.9 fusion.218
  45.2 3.1 fusion.224
  48.3 2.9 fusion.220
  73.2 2.9 fusion.218
  80.0 3.1 fusion.224
  83.1 2.9 fusion.220
  108.0 2.9 fusion.218
  114.9 3.1 fusion.224
  117.9 2.9 fusion.220
  142.9 2.9 fusion.218
  149.7 3.1 fusion.224
  152.8 2.9 fusion.220
  161.4 190.9 %all-gather.5.cloned.1.call-done = f32[512,128,128]{2,1,0:T(8,128)} async-done(((f32[16,128,128]{2,1,0:T(8,128)}), f32[512,128,128]{2,1,0:T(8,128)}) %all-gather.5.cloned.1.call-update) | async-done | bytes 33554448 | tf_op jit(solution)/shard_map/all_gather | solution.py:12
  352.3 195.8 %all-gather.7.cloned.1.call-done = f32[512,128,128]{2,1,0:T(8,128)} async-done(((f32[16,128,128]{2,1,0:T(8,128)}), f32[512,128,128]{2,1,0:T(8,128)}) %all-gather.7.cloned.1.call-update) | async-done | bytes 33554448 | tf_op jit(solution)/shard_map/all_gather | solution.py:12
  548.2 82.0 %while.29 = (s32[]{:T(128)}, f32[16,128,128]{2,1,0:T(8,128)S(1)}, s32[]{:T(128)}, f32[32,16,128,128]{3,2,1,0:T(8,128)}, f32[32,16,128,128]{3,2,1,0:T(8,128)}, /*index=5*/s32[]{:T(128)}, s32[]{:T(128)}, s32[]{:T(128)}) while((s32[]{:T(128)}, f32[16,128,128]{2,1,0:T(8,128)S(1)}, s32[]{:T(128)}, f32[32,16,128,128]{3,2,1,0:T(8,128)}, ...), condition=%wide.region_6.7_spmd, body=%wide.region_5.6_spmd.sunk | while | flops 402915328 | bytes 6292607 | solution.py:20
  548.4 2.8 convolution_add_fusion.7
  551.3 2.7 convolution_add_fusion.7
  554.1 2.7 convolution_add_fusion.7
  556.9 2.7 convolution_add_fusion.7
  559.7 2.7 convolution_add_fusion.7
  562.6 2.7 convolution_add_fusion.7
  565.4 2.7 convolution_add_fusion.7
  568.2 2.7 convolution_add_fusion.7
  571.0 2.7 convolution_add_fusion.7
  573.9 2.7 convolution_add_fusion.7
  576.7 2.7 convolution_add_fusion.7
  579.5 2.7 convolution_add_fusion.7
  582.3 2.7 convolution_add_fusion.7
  585.2 2.7 convolution_add_fusion.7
  588.0 2.7 convolution_add_fusion.7
  590.8 2.7 convolution_add_fusion.7
  593.6 2.7 convolution_add_fusion.7
  596.5 2.7 convolution_add_fusion.7
  599.3 2.7 convolution_add_fusion.7
  602.1 2.7 convolution_add_fusion.7
  604.9 2.7 convolution_add_fusion.7
  607.8 2.7 convolution_add_fusion.7
  610.6 2.7 convolution_add_fusion.7
  613.4 2.7 convolution_add_fusion.7
  616.2 2.7 convolution_add_fusion.7
  619.1 2.7 convolution_add_fusion.7
  621.9 2.7 convolution_add_fusion.7
  624.7 2.7 convolution_add_fusion.7
  627.5 2.7 convolution_add_fusion.7
  630.3 3.4 fusion.62
  633.7 4.4 multiply_reduce_fusion
  640.1 125.9 %all-reduce.2.cloned.1.call-done = f32[2048,128]{1,0:T(8,128)} async-done(((f32[2048,128]{1,0:T(8,128)}), f32[2048,128]{1,0:T(8,128)}) %all-reduce.2.cloned.1.call-update) | async-done | bytes 1048592 | tf_op jit(solution)/shard_map/psum | solution.py:25
  (211 shorter events, 124.1 us)
Async XLA Ops:
  7.2 345.1 %all-gather.5.cloned.1.call-start = ((), (), s32[]{:S(2)}) async-start(), calls=%async_computation.1 | async-start | bytes 34603008 | tf_op jit(solution)/shard_map/all_gather | solution.py:12
  9.8 0.7 copy-start.6
  9.8 1.2 copy-start.4
  11.7 1.5 copy-start.5
  35.0 3.4 copy-start
  41.5 3.7 copy-start.1
  69.9 3.3 copy-start
  76.3 3.7 copy-start.1
  104.7 3.4 copy-start
  111.1 3.7 copy-start.1
  139.5 3.4 copy-start
  145.9 3.7 copy-start.1
  157.9 1.6 copy-start.3
  157.9 390.2 %all-gather.7.cloned.1.call-start = ((), (), s32[]{:S(2)}) async-start(), calls=%async_computation.2 | async-start | bytes 34603008 | tf_op jit(solution)/shard_map/all_gather | solution.py:12
  158.7 607.3 %all-reduce.2.cloned.1.call-start = ((), (), s32[]{:S(2)}) async-start(), calls=%async_computation | async-start | bytes 2097152 | tf_op jit(solution)/shard_map/psum | solution.py:25
  548.2 82.0 %copy-start.2 = (f32[16,128,128]{2,1,0:T(8,128)S(1)}, f32[16,128,128]{2,1,0:T(8,128)}, u32[]{:S(2)}) copy-start(f32[16,128,128]{2,1,0:T(8,128)} %get-tuple-element.104) | copy-start | bytes 3145732
  633.7 4.4 copy-start.7
Sparse Core Ops, SparseCore 0:
  158.1 194.1 all-gather.4
  355.1 192.9 all-gather.6
  633.8 132.1 all-reduce.1
where the time goes:
time: 781 us; the launch traced here: 774 us
  waiting for transfers between devices  513 us (66%)
  matrix products  207 us (27%)
  local copies, waits for them, and re-layouts  26.8 us (3%)
  between operations  14 us (2%)
  other arithmetic  10.7 us (1%)
    all_gather x2, waiting for transfers between devices, entering(): gathered = jax.tree.map(lambda a: lax.all_gather(a, axis), part)  387 us
    dot_general x115, matrix products, matrix_product(): return jnp.einsum(form, left, right, precision=lax.Precision.HIGHEST)  207 us
    psum x1, waiting for transfers between devices, broadcast(): return lax.psum(kept, axis)  126 us
  transfers between devices with their start and end apart: 3, of which 3 were waited for; matrix products, arithmetic and copies ran while one was open for 1% of the time, Pallas kernels for 0%

commit v1 on v0

v1 whole, which is shorter than its diff:
```python
import functools

import jax
import jax.numpy as jnp
from jax import lax
from jax.experimental import pallas as pl
from jax.experimental.pallas import tpu as pltpu
from jax.sharding import PartitionSpec as P

DK = 128
HALF = 128
F32 = jnp.float32
BF16 = jnp.bfloat16
ROWS_BY_ROWS = (((1,), (1,)), ((), ()))
DOWN = (((0,), (0,)), ((), ()))
PLAIN = (((1,), (0,)), ((), ()))


def cut(a):
    high = a.astype(BF16)
    return high, (a - high.astype(F32)).astype(BF16)


def dot(left, right, dims=PLAIN):
    return lax.dot_general(left, right, dims, preferred_element_type=F32)


def dot3(left, right, dims=PLAIN):
    lh, ll = cut(left)
    rh, rl = cut(right)
    return dot(lh, rh, dims) + (dot(lh, rl, dims) + dot(ll, rh, dims))


def section_kernel(total, q_ref, k_ref, v_ref, ccol_ref, crow_ref, b_ref, ab_ref, o_ref, p_ref):
    tokens = q_ref.shape[0]
    group = v_ref.shape[1] // DK
    q = q_ref[...]
    k = k_ref[...]
    qf = q.astype(F32)
    kf = k.astype(F32)
    rq = lax.rsqrt(jnp.sum(qf * qf, axis=1, keepdims=True) + 1e-06) * DK ** (-0.5)
    rk = lax.rsqrt(jnp.sum(kf * kf, axis=1, keepdims=True) + 1e-06)
    rk_row = jnp.transpose(jnp.broadcast_to(rk, (tokens, DK)))[0:1, :]
    kk = dot(k, k, ROWS_BY_ROWS) * rk * rk_row
    qk = dot(q, k, ROWS_BY_ROWS) * rq * rk_row
    row = lax.broadcasted_iota(jnp.int32, (tokens, tokens), 0)
    col = lax.broadcasted_iota(jnp.int32, (tokens, tokens), 1)
    r = row[:HALF, :HALF]
    c = col[:HALF, :HALF]
    eye = (r == c).astype(F32)
    blocks = tokens // HALF
    lowers, xs = [], []
    data = []
    for w in range(group):
        ccol = ccol_ref[0, :, w : w + 1]
        crow = crow_ref[0, w : w + 1, :]
        beta = b_ref[0, :, w : w + 1]
        gap = jnp.where(row >= col, (ccol - crow) * (-1.0 / total), -1e30)
        mask = jnp.exp(gap)
        lower = jnp.where(row > col, kk * mask * beta, 0.0)
        grown = jnp.exp(ccol * (-1.0 / total))
        last = ccol[tokens - 1 : tokens, :]
        left = jnp.exp((last - ccol) * (-1.0 / total)) * rk
        final = jnp.exp(last * (-1.0 / total))
        right = jnp.concatenate(
            [kf * (rk * beta * grown), v_ref[:, w * DK : (w + 1) * DK].astype(F32) * beta], axis=1
        )
        data.append((lower, qk * mask, grown, left, final, right))
        for b in range(blocks):
            part = lower[b * HALF : (b + 1) * HALF, b * HALF : (b + 1) * HALF]
            lowers.append(part)
            xs.append(eye - jnp.where((r // 2) == (c // 2), part, 0.0))
    size = 2
    while size < HALF:
        inside = ((r // (2 * size)) == (c // (2 * size))) & ((r // size) != (c // size))
        cuts = [cut(x) for x in xs]
        mids = []
        for part, (xh, xl) in zip(lowers, cuts):
            mh, ml = cut(jnp.where(inside, part, 0.0))
            mids.append(dot(mh, xh) + (dot(mh, xl) + dot(ml, xh)))
        news = []
        for x, (xh, xl), mid in zip(xs, cuts, mids):
            yh, yl = cut(mid)
            news.append(x - (dot(xh, yh) + (dot(xh, yl) + dot(xl, yh))))
        xs = news
        size *= 2
    for w in range(group):
        lower, scores, grown, left, final, right = data[w]
        parts = []
        for b in range(blocks):
            rows = slice(b * HALF, (b + 1) * HALF)
            rhs = right[rows]
            for e in range(b):
                rhs = rhs - dot3(lower[rows, e * HALF : (e + 1) * HALF], parts[e])
            parts.append(dot3(xs[w * blocks + b], rhs))
        solved = jnp.concatenate(parts, axis=0)
        read = dot3(scores, solved)
        o_ref[w] = read[:, DK:]
        p_ref[w] = qf * (rq * grown) - read[:, :DK]
        sh, sl = cut(solved * left)
        moved = dot(k, sh, DOWN) + dot(k, sl, DOWN)
        ab_ref[w, :, :DK] = final * eye - moved[:, :DK]
        ab_ref[w, :, DK:] = moved[:, DK:]


def section(total, queries, keys, values, codes, beta):
    tokens, heads = codes.shape
    key_heads = queries.shape[1] // DK
    group = heads // key_heads
    sums = jnp.cumsum(codes, axis=0).astype(F32).reshape(tokens, key_heads, group)
    beta = (beta.astype(F32) / total).reshape(tokens, key_heads, group)
    col = lambda h: (0, h)
    lead = lambda h: (h, 0, 0)
    return pl.pallas_call(
        functools.partial(section_kernel, total),
        grid=(key_heads,),
        in_specs=[
            pl.BlockSpec((tokens, DK), col),
            pl.BlockSpec((tokens, DK), col),
            pl.BlockSpec((tokens, group * DK), col),
            pl.BlockSpec((1, tokens, group), lead),
            pl.BlockSpec((1, group, tokens), lead),
            pl.BlockSpec((1, tokens, group), lead),
        ],
        out_specs=[
            pl.BlockSpec((group, DK, 2 * DK), lead),
            pl.BlockSpec((group, tokens, DK), lead),
            pl.BlockSpec((group, tokens, DK), lead),
        ],
        out_shape=[
            jax.ShapeDtypeStruct((heads, DK, 2 * DK), F32),
            jax.ShapeDtypeStruct((heads, tokens, DK), F32),
            jax.ShapeDtypeStruct((heads, tokens, DK), F32),
        ],
        compiler_params=pltpu.CompilerParams(vmem_limit_bytes=40 * 1024 * 1024),
        name="section",
    )(
        queries,
        keys,
        values,
        jnp.transpose(sums, (1, 0, 2)),
        jnp.transpose(sums, (1, 2, 0)),
        jnp.transpose(beta, (1, 0, 2)),
    )


def total_kernel(ab_ref, out_ref):
    sections, heads = ab_ref.shape[:2]
    for h in range(heads):
        out_ref[h] = ab_ref[0, h]
    for s in range(1, sections):
        for h in range(heads):
            new = dot3(ab_ref[s, h, :, :DK], out_ref[h])
            out_ref[h, :, :DK] = new[:, :DK]
            out_ref[h, :, DK:] = new[:, DK:] + ab_ref[s, h, :, DK:]


def total_map(ab):
    return pl.pallas_call(
        total_kernel,
        out_shape=jax.ShapeDtypeStruct(ab.shape[1:], F32),
        compiler_params=pltpu.CompilerParams(vmem_limit_bytes=40 * 1024 * 1024),
        name="total",
    )(ab)


def enter_kernel(place_ref, ab_ref, all_ref, enter_ref, final_ref):
    sections, heads = ab_ref.shape[:2]
    planes = all_ref.shape[0]
    place = place_ref[0]
    for h in range(heads):
        state = jnp.zeros((DK, DK), F32)
        mine = state
        for z in range(planes):
            mine = jnp.where(place == z, state, mine)
            later = all_ref[z, h, :, DK:]
            state = later if z == 0 else dot3(all_ref[z, h, :, :DK], state) + later
        final_ref[h] = state
        enter_ref[0, h] = mine
    for s in range(1, sections):
        for h in range(heads):
            enter_ref[s, h] = (
                dot3(ab_ref[s - 1, h, :, :DK], enter_ref[s - 1, h]) + ab_ref[s - 1, h, :, DK:]
            )


def enter(place, ab, every):
    sections, heads = ab.shape[:2]
    vmem = pl.BlockSpec(memory_space=pltpu.VMEM)
    return pl.pallas_call(
        enter_kernel,
        in_specs=[pl.BlockSpec(memory_space=pltpu.SMEM), vmem, vmem],
        out_specs=[vmem, vmem],
        out_shape=[
            jax.ShapeDtypeStruct((sections, heads, DK, DK), F32),
            jax.ShapeDtypeStruct((heads, DK, DK), F32),
        ],
        compiler_params=pltpu.CompilerParams(vmem_limit_bytes=40 * 1024 * 1024),
        name="enter",
    )(place, ab, every)


def output_kernel(o_ref, p_ref, s_ref, gain_ref, out_ref):
    for w in range(o_ref.shape[0]):
        o = o_ref[w] + dot3(p_ref[w], s_ref[w])
        scale = lax.rsqrt(jnp.mean(o * o, axis=1, keepdims=True) + 1e-06)
        out_ref[:, w * DK : (w + 1) * DK] = (o * scale * gain_ref[...]).astype(BF16)


def output(own, reach, state, gain, group):
    heads, tokens, _ = own.shape
    lead = lambda h: (h, 0, 0)
    return pl.pallas_call(
        output_kernel,
        grid=(heads // group,),
        in_specs=[
            pl.BlockSpec((group, tokens, DK), lead),
            pl.BlockSpec((group, tokens, DK), lead),
            pl.BlockSpec((group, DK, DK), lead),
            pl.BlockSpec((1, DK), lambda h: (0, 0)),
        ],
        out_specs=pl.BlockSpec((tokens, group * DK), lambda h: (0, h)),
        out_shape=jax.ShapeDtypeStruct((tokens, heads * DK), BF16),
        compiler_params=pltpu.CompilerParams(vmem_limit_bytes=40 * 1024 * 1024),
        name="output",
    )(own, reach, state, gain.reshape(1, DK))


def shards(queries, keys, values, gate_codes, beta_codes, norm_gain):
    tokens, heads = gate_codes.shape
    sections = lax.axis_size("sec")
    place = lax.axis_index("sec")
    total = tokens * sections
    plane = 8
    planes = sections // plane
    kept = heads // plane
    ab, own, reach = section(total, queries, keys, values, gate_codes, beta_codes)
    near = [[z * plane + r for r in range(plane)] for z in range(planes)]
    far = [[z * plane + r for z in range(planes)] for r in range(plane)]
    ab = lax.all_to_all(
        ab.reshape(plane, kept, DK, 2 * DK), "sec", 0, 0, axis_index_groups=near, tiled=True
    )
    every = lax.all_gather(total_map(ab), "sec", axis_index_groups=far)
    z, r = place // plane, place % plane
    entering, final = enter(z.reshape(1), ab, every)
    rows = heads * DK // sections
    span = kept * DK
    final = final.reshape(span, DK)
    starts = [(z * plane + d) * rows - r * span for d in range(plane)]
    ends = jnp.stack([lax.dynamic_slice_in_dim(final, jnp.clip(s, 0, span - rows), rows, 0) for s in starts])
    back = lax.all_to_all(
        jnp.concatenate([entering.reshape(plane, span, DK), ends], axis=1),
        "sec", 0, 0, axis_index_groups=near, tiled=True,
    )
    state = back[:, :span].reshape(heads, DK, DK)
    owner = (place * rows) // span
    final_state = lax.dynamic_index_in_dim(back[:, span:], owner, 0, False)
    group = heads // (queries.shape[1] // DK)
    return output(own, reach, state, norm_gain, group), final_state


def solution(mesh):
    rows = P(("parts", "sec"), None)
    return jax.shard_map(
        shards,
        mesh=mesh,
        in_specs=(rows, rows, rows, rows, rows, P()),
        out_specs=(rows, rows),
        check_vma=False,
    )
```

time: 781 us -> 149 us (0.19)
  the two profiles are of different devices: /device:TPU:29 before, /device:TPU:0 now
where the time goes in v1:
time: 149 us; the launch traced here: 148 us
  waiting for transfers between devices  45.6 us (31%)
  Pallas kernels  43.3 us (29%)
  blocking collectives  31.6 us (21%)
  between operations  14.3 us (10%)
  local copies, waits for them, and re-layouts  7.35 us (5%)
  starting transfers between devices  3.69 us (2%)
  other arithmetic  2.59 us (2%)
    pallas_call x1, Pallas kernels, section(): pl.pallas_call(functools.partial(section_kernel, total), grid=(key_heads,...  34.5 us
    all_to_all x1, blocking collectives, shards(): lax.all_to_all(ab.reshape(plane, kept, DK, 2 * DK), 'sec', 0, 0, axis_ind...  31.6 us
    all_gather x1, waiting for transfers between devices, shards(): every = lax.all_gather(total_map(ab), 'sec', axis_index_groups=far)  27.4 us
    all_to_all x1, waiting for transfers between devices, shards(): lax.all_to_all(jnp.concatenate([entering.reshape(plane, span, DK), ends],...  18.2 us
    unnamed x27, local copies, waits for them, and re-layouts  5.67 us
    pallas_call x1, Pallas kernels, output(): pl.pallas_call(output_kernel, grid=(heads // group,), in_specs=[pl.BlockS...  4.5 us
    all_to_all x1, starting transfers between devices, shards(): lax.all_to_all(jnp.concatenate([entering.reshape(plane, span, DK), ends],...  3.65 us
  transfers between devices with their start and end apart: 2, of which 2 were waited for; matrix products, arithmetic and copies ran while one was open for 0% of the time, Pallas kernels for 0%

profile of v1, /device:TPU:0, one launch (start us, length us, event | category | flops | bytes accessed | tf_op | source)
XLA Modules:
  0.0 148.4 jit_solution(5623492857204994105)
XLA Ops:
  7.2 0.0 copy-start
  7.2 0.0 copy-start.6
  7.2 0.0 all-gather.3.cloned.1.call-start
  7.2 0.7 copy-done
  7.9 0.6 reduce-window.6
  8.5 0.2 slice_reduce_fusion
  8.7 0.1 bitcast_bitcast_fusion
  8.8 0.4 copy.17.ccol_ref
  9.2 0.7 convert_multiply_fusion
  9.9 0.4 copy.16
  10.3 0.0 copy-done.6
  10.3 0.0 copy-start.7
  10.3 1.0 copy-done.7
  11.3 0.0 copy-start.8
  11.3 1.0 copy-done.8
  12.4 34.5 %section.1 = (f32[16,128,256]{2,1,0:T(8,128)S(1)}, f32[16,256,128]{2,1,0:T(8,128)S(1)}, f32[16,256,128]{2,1,0:T(8,128)S(1)}) custom-call(bf16[256,1024]{1,0:T(8,128)(2,1)S(1)} %copy-done.7, bf16[256,1024]{1,0:T(8,128)(2,1)S(1)} %copy-done.8, bf16[256,2048]{1,0:T(8,128)(2,1)S(1)} %copy-done.6, f32[8,256,2]{2,1,0:T(8,128)S(1)} %copy.17.ccol_ref, ...), custom_call_target="tpu_custom_call" | custom-call | tf_op jit(solution)/shard_map/section/pallas_call | solution.py:114
  46.9 0.0 copy-start.1
  46.9 0.0 copy-start.3
  46.9 31.6 %all_to_all.10.ab_ref = f32[8,2,128,256]{3,2,1,0:T(8,128)S(1)} all-to-all(f32[8,2,128,256]{3,2,1,0:T(8,128)S(1)} %bitcast.47), channel_id=1, replica_groups={{0,1,2,3,4,5,6,7},{8,9,10,11,12,13,14,15},{16,17,18,19,20,21,22,23},{24..., dimensions={0} | all-to-all | bytes 4194304 | tf_op jit(solution)/shard_map/all_to_all | solution.py:240
  78.5 0.0 copy-done.1
  78.5 0.0 copy-done.3
  78.5 2.4 %total.1 = f32[2,128,256]{2,1,0:T(8,128)} custom-call(f32[8,2,128,256]{3,2,1,0:T(8,128)S(1)} %all_to_all.10.ab_ref), custom_call_target="tpu_custom_call" | custom-call | tf_op jit(solution)/shard_map/total/pallas_call | solution.py:159
  80.9 0.0 all-gather.3.cloned.1.call-update
  81.0 27.4 %all-gather.3.cloned.1.call-done = f32[8,128,256]{2,1,0:T(8,128)} async-done(((f32[2,128,256]{2,1,0:T(8,128)}), f32[8,128,256]{2,1,0:T(8,128)}) %all-gather.3.cloned.1.call-update) | async-done | bytes 1048592 | tf_op jit(solution)/shard_map/all_gather | solution.py:243
  108.4 0.0 copy-start.5
  108.4 1.2 copy-done.5
  109.6 1.8 %enter.1 = (f32[8,2,128,128]{3,2,1,0:T(8,128)S(1)}, f32[2,128,128]{2,1,0:T(8,128)S(1)}) custom-call(s32[1]{0:T(128)} %bitcast.5.place_ref, f32[8,2,128,256]{3,2,1,0:T(8,128)S(1)} %all_to_all.10.ab_ref, f32[4,2,128,256]{3,2,1,0:T(8,128)S(1)} %bitcast.48), custom_call_target="tpu_custom_call" | custom-call | tf_op jit(solution)/shard_map/enter/pallas_call | solution.py:190
  111.6 1.2 pad_maximum_fusion
  112.8 3.7 %all-to-all-start.1 = ((f32[8,320,128]{2,1,0:T(8,128)}), f32[8,320,128]{2,1,0:T(8,128)S(1)}, u32[]{:S(2)}, u32[]{:S(2)}) async-start(f32[8,320,128]{2,1,0:T(8,128)} %pad_maximum_fusion), calls=%async_computation.1 | async-start | bytes 2621440 | tf_op jit(solution)/shard_map/all_to_all | solution.py:251
  116.5 0.0 copy-start.2
  116.5 0.0 copy-start.9
  116.5 18.2 %all-to-all-done.1 = f32[8,320,128]{2,1,0:T(8,128)S(1)} async-done(((f32[8,320,128]{2,1,0:T(8,128)}), f32[8,320,128]{2,1,0:T(8,128)S(1)}, u32[]{:S(2)}, u32[]{:S(2)}) %all-to-all-start.1) | async-done | bytes 1310752 | tf_op jit(solution)/shard_map/all_to_all | solution.py:251
  134.7 0.6 dynamic-slice_bitcast_fusion
  135.3 0.1 slice.17
  135.4 0.0 copy-done.2
  135.4 0.0 copy-done.9
  135.4 0.0 copy-start.4
  135.4 1.6 %copy-done.4 = f32[16,256,128]{2,1,0:T(8,128)S(1)} copy-done((f32[16,256,128]{2,1,0:T(8,128)S(1)}, f32[16,256,128]{2,1,0:T(8,128)}, u32[]{:S(2)}) %copy-start.4) | copy-done | bytes 2097176
  137.0 4.5 %output.1 = bf16[256,2048]{1,0:T(8,128)(2,1)} custom-call(f32[16,256,128]{2,1,0:T(8,128)S(1)} %copy-done.2, f32[16,256,128]{2,1,0:T(8,128)S(1)} %copy-done.4, f32[16,128,128]{2,1,0:T(8,128)S(1)} %bitcast.45, f32[1,128]{1,0:T(1,128)S(1)} %bitcast.60), custom_call_target="tpu_custom_call" | custom-call | tf_op jit(solution)/shard_map/output/pallas_call | solution.py:213
  (14 shorter events, 0.2 us)
Async XLA Ops:
  7.2 0.7 copy-start
  7.2 3.1 %copy-start.6 = (bf16[256,2048]{1,0:T(8,128)(2,1)S(1)}, bf16[256,2048]{1,0:T(8,128)(2,1)}, u32[]{:S(2)}) copy-start(bf16[256,2048]{1,0:T(8,128)(2,1)} %v_ref.1) | copy-start | bytes 3145732
  7.2 101.2 %all-gather.3.cloned.1.call-start = ((), (), s32[]{:S(2)}) async-start(), calls=%async_computation.2 | async-start | bytes 1310720 | tf_op jit(solution)/shard_map/all_gather | solution.py:243
  10.3 1.0 copy-start.7
  11.3 1.0 copy-start.8
  46.9 31.6 %copy-start.1 = (f32[16,256,128]{2,1,0:T(8,128)}, f32[16,256,128]{2,1,0:T(8,128)S(1)}, u32[]{:S(2)}) copy-start(f32[16,256,128]{2,1,0:T(8,128)S(1)} %get-tuple-element.7.o_ref) | copy-start | bytes 6291460
  46.9 31.6 %copy-start.3 = (f32[16,256,128]{2,1,0:T(8,128)}, f32[16,256,128]{2,1,0:T(8,128)S(1)}, u32[]{:S(2)}) copy-start(f32[16,256,128]{2,1,0:T(8,128)S(1)} %get-tuple-element.8.p_ref) | copy-start | bytes 6291460
  108.4 1.2 copy-start.5
  112.8 21.9 %all-to-all-start.1 = ((f32[8,320,128]{2,1,0:T(8,128)}), f32[8,320,128]{2,1,0:T(8,128)S(1)}, u32[]{:S(2)}, u32[]{:S(2)}) async-start(f32[8,320,128]{2,1,0:T(8,128)} %pad_maximum_fusion), calls=%async_computation.1 | async-start | bytes 2621440 | tf_op jit(solution)/shard_map/all_to_all | solution.py:251
  116.5 18.9 %copy-start.2 = (f32[16,256,128]{2,1,0:T(8,128)S(1)}, f32[16,256,128]{2,1,0:T(8,128)}, u32[]{:S(2)}) copy-start(f32[16,256,128]{2,1,0:T(8,128)} %copy-done.1) | copy-start | bytes 6291460
  116.5 18.9 %copy-start.9 = (f32[128]{0:T(128)S(1)}, f32[128]{0:T(128)}, u32[]{:S(2)}) copy-start(f32[128]{0:T(128)} %param.11) | copy-start | bytes 1540
  135.4 1.6 %copy-start.4 = (f32[16,256,128]{2,1,0:T(8,128)S(1)}, f32[16,256,128]{2,1,0:T(8,128)}, u32[]{:S(2)}) copy-start(f32[16,256,128]{2,1,0:T(8,128)} %copy-done.3) | copy-start | bytes 6291460
Sparse Core Ops, SparseCore 0:
  81.0 27.2 all-gather.2

commit v2 on v1

v2 whole, which is shorter than its diff:
```python
import functools

import jax
import jax.numpy as jnp
from jax import lax
from jax.experimental import pallas as pl
from jax.experimental.pallas import tpu as pltpu
from jax.sharding import PartitionSpec as P

DK = 128
HALF = 128
F32 = jnp.float32
BF16 = jnp.bfloat16
ROWS_BY_ROWS = (((1,), (1,)), ((), ()))
DOWN = (((0,), (0,)), ((), ()))
PLAIN = (((1,), (0,)), ((), ()))


def cut(a):
    high = a.astype(BF16)
    return high, (a - high.astype(F32)).astype(BF16)


def dot(left, right, dims=PLAIN):
    return lax.dot_general(left, right, dims, preferred_element_type=F32)


def dot3(left, right, dims=PLAIN):
    lh, ll = cut(left)
    rh, rl = cut(right)
    return dot(lh, rh, dims) + (dot(lh, rl, dims) + dot(ll, rh, dims))


def section_map(total, h, q_ref, k_ref, v_ref, ccol_ref, crow_ref, b_ref, ab_ref, o_ref, p_ref):
    tokens = q_ref.shape[0]
    key_heads = q_ref.shape[1] // DK
    group = v_ref.shape[1] // DK // key_heads
    q = q_ref[:, pl.ds(pl.multiple_of(h * DK, DK), DK)]
    k = k_ref[:, pl.ds(pl.multiple_of(h * DK, DK), DK)]
    v = v_ref[:, pl.ds(pl.multiple_of(h * group * DK, DK), group * DK)]
    ccols, crows, betas = ccol_ref[h], crow_ref[h], b_ref[h]
    qf = q.astype(F32)
    kf = k.astype(F32)
    rq = lax.rsqrt(jnp.sum(qf * qf, axis=1, keepdims=True) + 1e-06) * DK ** (-0.5)
    rk = lax.rsqrt(jnp.sum(kf * kf, axis=1, keepdims=True) + 1e-06)
    rk_row = jnp.transpose(jnp.broadcast_to(rk, (tokens, DK)))[0:1, :]
    kk = dot(k, k, ROWS_BY_ROWS) * rk * rk_row
    qk = dot(q, k, ROWS_BY_ROWS) * rq * rk_row
    row = lax.broadcasted_iota(jnp.int32, (tokens, tokens), 0)
    col = lax.broadcasted_iota(jnp.int32, (tokens, tokens), 1)
    r = row[:HALF, :HALF]
    c = col[:HALF, :HALF]
    eye = (r == c).astype(F32)
    blocks = tokens // HALF
    lowers, xs, data = [], [], []
    for w in range(group):
        ccol = ccols[:, w : w + 1]
        crow = crows[w : w + 1, :]
        beta = betas[:, w : w + 1]
        gap = jnp.where(row >= col, (ccol - crow) * (-1.0 / total), -1e30)
        mask = jnp.exp(gap)
        lower = jnp.where(row > col, kk * mask * beta, 0.0)
        grown = jnp.exp(ccol * (-1.0 / total))
        last = ccol[tokens - 1 : tokens, :]
        left = jnp.exp((last - ccol) * (-1.0 / total)) * rk
        final = jnp.exp(last * (-1.0 / total))
        right = jnp.concatenate(
            [kf * (rk * beta * grown), v[:, w * DK : (w + 1) * DK].astype(F32) * beta], axis=1
        )
        data.append((lower, qk * mask, grown, left, final, right))
        for b in range(blocks):
            part = lower[b * HALF : (b + 1) * HALF, b * HALF : (b + 1) * HALF]
            lowers.append(part)
            xs.append(eye - jnp.where((r >> 1) == (c >> 1), part, 0.0))
    bit = 1
    while (1 << bit) < HALF:
        inside = ((r >> (bit + 1)) == (c >> (bit + 1))) & ((r >> bit) != (c >> bit))
        cuts = [cut(x) for x in xs]
        mids = []
        for part, (xh, xl) in zip(lowers, cuts):
            mh, ml = cut(jnp.where(inside, part, 0.0))
            mids.append(dot(mh, xh) + (dot(mh, xl) + dot(ml, xh)))
        news = []
        for x, (xh, xl), mid in zip(xs, cuts, mids):
            yh, yl = cut(mid)
            news.append(x - (dot(xh, yh) + (dot(xh, yl) + dot(xl, yh))))
        xs = news
        bit += 1
    for w in range(group):
        lower, scores, grown, left, final, right = data[w]
        parts = []
        for b in range(blocks):
            rows = slice(b * HALF, (b + 1) * HALF)
            rhs = right[rows]
            for e in range(b):
                rhs = rhs - dot3(lower[rows, e * HALF : (e + 1) * HALF], parts[e])
            parts.append(dot3(xs[w * blocks + b], rhs))
        solved = jnp.concatenate(parts, axis=0)
        read = dot3(scores, solved)
        o_ref[h, w] = read[:, DK:]
        p_ref[h, w] = qf * (rq * grown) - read[:, :DK]
        sh, sl = cut(solved * left)
        moved = dot(k, sh, DOWN) + dot(k, sl, DOWN)
        ab_ref[h, w, :, :DK] = final * eye - moved[:, :DK]
        ab_ref[h, w, :, DK:] = moved[:, DK:]


def kernel(
    total, sections,
    q_ref, k_ref, v_ref, ccol_ref, crow_ref, b_ref, gain_ref, out_ref, last_ref,
    ab, recv, o_ref, p_ref, sin, sout, ent, st, fin,
    map_send, map_recv, chain_send, chain_recv, ret_send, ret_recv, fin_send, fin_recv,
):
    plane = q_ref.shape[1] // DK
    planes = sections // plane
    kept = ab.shape[1]
    rows = fin.shape[0]
    place = lax.axis_index("sec")
    z, r = place // plane, place % plane
    base = z * plane
    owner = (planes - 1) * plane + place // planes

    def remote(src, dst, send, receive, target):
        return pltpu.make_async_remote_copy(
            src_ref=src, dst_ref=dst, send_sem=send, recv_sem=receive,
            device_id={"sec": target}, device_id_type=pl.DeviceIdType.MESH,
        )

    def greet(target):
        pl.semaphore_signal(
            barrier, inc=1, device_id={"sec": target}, device_id_type=pl.DeviceIdType.MESH
        )

    barrier = pltpu.get_barrier_semaphore()
    for i in range(1, plane):
        greet(base + (r + i) % plane)
    pl.when(z > 0)(lambda: greet(place - plane))
    pl.when(owner != place)(lambda: greet(owner))
    at_end = z == planes - 1
    holders = planes - jnp.where(owner == place, 1, 0)
    expected = plane - 1 + jnp.where(at_end, holders, 1)

    def send_map(h):
        return remote(ab.at[h], recv.at[r], map_send.at[h], map_recv.at[r], base + h)

    def one_head(i, carry):
        h = (r + 1 + i) % plane
        section_map(total, h, q_ref, k_ref, v_ref, ccol_ref, crow_ref, b_ref, ab, o_ref, p_ref)
        pl.when(i == 0)(lambda: pl.semaphore_wait(barrier, expected))
        pl.when(i < plane - 1)(lambda: send_map(h).start())
        return carry

    lax.fori_loop(0, plane, one_head, 0)
    recv[r] = ab[r]

    for s in range(plane):

        @pl.when(r != s)
        def _(s=s):
            remote(ab.at[s], recv.at[s], map_send.at[s], map_recv.at[s], base + s).wait_recv()

        if s > 0:
            for e in range(kept):
                later = recv[s, e, :, :DK]
                new = dot3(later, recv[s - 1, e])
                recv[s, e, :, :DK] = new[:, :DK]
                recv[s, e, :, DK:] = new[:, DK:] + recv[s, e, :, DK:]

    def chain(e, target):
        return remote(
            sout.at[pl.ds(e * DK, DK)], sin.at[e], chain_send.at[e], chain_recv.at[e], target
        )

    @pl.when(z == 0)
    def _():
        sin[...] = jnp.zeros_like(sin)

    for e in range(kept):

        @pl.when(z > 0)
        def _(e=e):
            chain(e, place - plane).wait_recv()

        sout[e * DK : (e + 1) * DK] = (
            dot3(recv[plane - 1, e, :, :DK], sin[e]) + recv[plane - 1, e, :, DK:]
        )

        @pl.when(z < planes - 1)
        def _(e=e):
            chain(e, place + plane).start()

    def back(s):
        return remote(ent.at[s], st.at[r], ret_send.at[s], ret_recv.at[r], base + s)

    for s in range(plane):
        for e in range(kept):
            if s == 0:
                ent[s, e] = sin[e]
            else:
                ent[s, e] = dot3(recv[s - 1, e, :, :DK], sin[e]) + recv[s - 1, e, :, DK:]
        pl.when(r != s)(lambda s=s: back(s).start())
    st[r] = ent[r]

    def last_rows(c):
        return remote(
            sout.at[pl.ds(c * rows, rows)], fin, fin_send.at[c], fin_recv, r * planes + c
        )

    for c in range(planes):
        pl.when(at_end & (r * planes + c != place))(lambda c=c: last_rows(c).start())

        @pl.when(at_end & (r * planes + c == place))
        def _(c=c):
            fin[...] = sout[c * rows : (c + 1) * rows]

    def read_out(i, carry):
        h = (r + i) % plane

        @pl.when(i > 0)
        def _():
            remote(ent.at[h], st.at[h], ret_send.at[h], ret_recv.at[h], base + h).wait_recv()

        for w in range(kept):
            o = o_ref[h, w] + dot3(p_ref[h, w], st[h, w])
            scale = lax.rsqrt(jnp.mean(o * o, axis=1, keepdims=True) + 1e-06)
            columns = pl.ds(pl.multiple_of((h * kept + w) * DK, DK), DK)
            out_ref[:, columns] = (o * scale * gain_ref[...]).astype(BF16)
        return carry

    lax.fori_loop(0, plane, read_out, 0)

    @pl.when(owner != place)
    def _():
        remote(sout.at[pl.ds(0, rows)], fin, fin_send.at[0], fin_recv, owner).wait_recv()

    last_ref[...] = fin[...]

    for s in range(plane):

        @pl.when(r != s)
        def _(s=s):
            send_map(s).wait_send()
            back(s).wait_send()

    for e in range(kept):
        pl.when(z < planes - 1)(lambda e=e: chain(e, place + plane).wait_send())
    for c in range(planes):
        pl.when(at_end & (r * planes + c != place))(lambda c=c: last_rows(c).wait_send())


def shards(queries, keys, values, gate_codes, beta_codes, norm_gain):
    tokens, heads = gate_codes.shape
    sections = lax.axis_size("sec")
    total = tokens * sections
    plane = queries.shape[1] // DK
    planes = sections // plane
    kept = heads // plane
    rows = heads * DK // sections
    sums = jnp.cumsum(gate_codes, axis=0).astype(F32).reshape(tokens, plane, kept)
    beta = (beta_codes.astype(F32) / total).reshape(tokens, plane, kept)
    vmem = pl.BlockSpec(memory_space=pltpu.VMEM)
    dma = pltpu.SemaphoreType.DMA
    return pl.pallas_call(
        functools.partial(kernel, total, sections),
        in_specs=[vmem] * 7,
        out_specs=[vmem] * 2,
        out_shape=[
            jax.ShapeDtypeStruct((tokens, heads * DK), BF16),
            jax.ShapeDtypeStruct((rows, DK), F32),
        ],
        scratch_shapes=[
            pltpu.VMEM((plane, kept, DK, 2 * DK), F32),
            pltpu.VMEM((plane, kept, DK, 2 * DK), F32),
            pltpu.VMEM((plane, kept, tokens, DK), F32),
            pltpu.VMEM((plane, kept, tokens, DK), F32),
            pltpu.VMEM((kept, DK, DK), F32),
            pltpu.VMEM((kept * DK, DK), F32),
            pltpu.VMEM((plane, kept, DK, DK), F32),
            pltpu.VMEM((plane, kept, DK, DK), F32),
            pltpu.VMEM((rows, DK), F32),
            dma((plane,)), dma((plane,)), dma((kept,)), dma((kept,)),
            dma((plane,)), dma((plane,)), dma((planes,)), dma,
        ],
        compiler_params=pltpu.CompilerParams(
            vmem_limit_bytes=48 * 1024 * 1024, collective_id=0, has_side_effects=True
        ),
        name="recurrence",
    )(
        queries,
        keys,
        values,
        jnp.transpose(sums, (1, 0, 2)),
        jnp.transpose(sums, (1, 2, 0)),
        jnp.transpose(beta, (1, 0, 2)),
        norm_gain.reshape(1, DK),
    )


def solution(mesh):
    rows = P(("parts", "sec"), None)
    return jax.shard_map(
        shards,
        mesh=mesh,
        in_specs=(rows, rows, rows, rows, rows, P()),
        out_specs=(rows, rows),
        check_vma=False,
    )
```

time: 149 us -> 72.8 us (0.49)
  the two profiles are of different devices: /device:TPU:0 before, /device:TPU:29 now
where the time goes in v2:
time: 72.8 us; the launch traced here: 72.5 us
  Pallas kernels  64.6 us (89%)
  local copies, waits for them, and re-layouts  6.51 us (9%)
    pallas_call x1, Pallas kernels, shards(): pl.pallas_call(functools.partial(kernel, total, sections), in_specs=[vmem...  64.6 us
    unnamed x14, local copies, waits for them, and re-layouts  5.55 us

profile of v2, /device:TPU:29, one launch (start us, length us, event | category | flops | bytes accessed | tf_op | source)
XLA Modules:
  0.0 72.5 jit_solution(13789265763383460118)
XLA Ops:
  0.6 0.0 copy-start
  0.6 0.7 copy-done
  1.4 0.6 reduce-window.6
  1.9 0.2 slice_reduce_fusion
  2.2 0.1 bitcast_bitcast_fusion
  2.2 0.0 copy-start.5
  2.3 0.7 copy-done.5
  3.0 0.0 copy-start.1
  3.0 0.4 copy.12
  3.4 0.0 copy-start.4
  3.4 0.4 copy.13.ccol_ref
  3.8 0.5 copy-done.1
  4.2 0.0 copy-done.4
  4.2 0.0 copy-start.2
  4.2 1.0 %copy-done.2 = bf16[256,1024]{1,0:T(8,128)(2,1)S(1)} copy-done((bf16[256,1024]{1,0:T(8,128)(2,1)S(1)}, bf16[256,1024]{1,0:T(8,128)(2,1)}, u32[]{:S(2)}) %copy-start.2) | copy-done | bytes 524312
  5.3 0.0 copy-start.3
  5.3 1.0 %copy-done.3 = bf16[256,1024]{1,0:T(8,128)(2,1)S(1)} copy-done((bf16[256,1024]{1,0:T(8,128)(2,1)S(1)}, bf16[256,1024]{1,0:T(8,128)(2,1)}, u32[]{:S(2)}) %copy-start.3) | copy-done | bytes 524312
  6.3 64.6 %recurrence.1 = (bf16[256,2048]{1,0:T(8,128)(2,1)S(1)}, f32[64,128]{1,0:T(8,128)S(1)}) custom-call(bf16[256,1024]{1,0:T(8,128)(2,1)S(1)} %copy-done.2, bf16[256,1024]{1,0:T(8,128)(2,1)S(1)} %copy-done.3, bf16[256,2048]{1,0:T(8,128)(2,1)S(1)} %copy-done.1, f32[8,256,2]{2,1,0:T(8,128)S(1)} %copy.13.ccol_ref, f32[8,2,256]{2,1,0:T(2,128)S(1)} %bitcast.23, ...), custom_call_target="tpu_custom_call" | custom-call | tf_op jit(solution)/shard_map/recurrence/pallas_call | solution.py:263
  70.9 1.0 %copy.20 = bf16[256,2048]{1,0:T(8,128)(2,1)} copy(bf16[256,2048]{1,0:T(8,128)(2,1)S(1)} %get-tuple-element.4) | data formatting | bytes 2097152
  71.9 0.6 copy.21
  (6 shorter events, 0.1 us)
Async XLA Ops:
  0.6 0.7 copy-start
  2.2 0.7 %copy-start.5 = (s32[256,16]{0,1:T(8,128)S(1)}, s32[256,16]{0,1:T(8,128)}, u32[]{:S(2)}) copy-start(s32[256,16]{0,1:T(8,128)} %param.10) | copy-start | bytes 49156
  3.0 1.2 %copy-start.1 = (bf16[256,2048]{1,0:T(8,128)(2,1)S(1)}, bf16[256,2048]{1,0:T(8,128)(2,1)}, u32[]{:S(2)}) copy-start(bf16[256,2048]{1,0:T(8,128)(2,1)} %v_ref.1) | copy-start | bytes 3145732
  3.4 0.8 %copy-start.4 = (f32[128]{0:T(128)S(1)}, f32[128]{0:T(128)}, u32[]{:S(2)}) copy-start(f32[128]{0:T(128)} %param.11) | copy-start | bytes 1540
  4.2 1.0 %copy-start.2 = (bf16[256,1024]{1,0:T(8,128)(2,1)S(1)}, bf16[256,1024]{1,0:T(8,128)(2,1)}, u32[]{:S(2)}) copy-start(bf16[256,1024]{1,0:T(8,128)(2,1)} %q_ref.1) | copy-start | bytes 1572868
  5.3 1.0 %copy-start.3 = (bf16[256,1024]{1,0:T(8,128)(2,1)S(1)}, bf16[256,1024]{1,0:T(8,128)(2,1)}, u32[]{:S(2)}) copy-start(bf16[256,1024]{1,0:T(8,128)(2,1)} %k_ref.1) | copy-start | bytes 1572868

commit v3 on v2

--- a/solution.py
+++ b/solution.py
@@ -25,10 +25,20 @@
     return lax.dot_general(left, right, dims, preferred_element_type=F32)
 
 
-def dot3(left, right, dims=PLAIN):
-    lh, ll = cut(left)
-    rh, rl = cut(right)
-    return dot(lh, rh, dims) + (dot(lh, rl, dims) + dot(ll, rh, dims))
+def product(left, right):
+    (lh, ll), (rh, rl) = left, right
+    if lh.shape[1] > DK:
+        return dot(lh, rh) + (dot(lh, rl) + dot(ll, rh))
+    wide = jnp.concatenate([lh, ll], axis=1)
+    if rh.shape[1] > DK:
+        return dot(wide, jnp.concatenate([rh, rh], axis=0)) + dot(lh, rl)
+    both = jnp.concatenate([rh, rl], axis=1)
+    halves = dot(wide, jnp.concatenate([both, both], axis=0))
+    return halves[:, :DK] + halves[:, DK:]
+
+
+def dot3(left, right):
+    return product(cut(left), cut(right))
 
 
 def section_map(total, h, q_ref, k_ref, v_ref, ccol_ref, crow_ref, b_ref, ab_ref, o_ref, p_ref):
@@ -71,20 +81,24 @@
         for b in range(blocks):
             part = lower[b * HALF : (b + 1) * HALF, b * HALF : (b + 1) * HALF]
             lowers.append(part)
-            xs.append(eye - jnp.where((r >> 1) == (c >> 1), part, 0.0))
-    bit = 1
+    near = (r >> 4) == (c >> 4)
+    ns = [jnp.where(near, part, 0.0) for part in lowers]
+    seconds = [product(x, x) for x in map(cut, ns)]
+    cuts = [cut(x) for x in seconds]
+    both = [product(cut(jnp.concatenate([n, f], axis=0)), x) for n, f, x in zip(ns, seconds, cuts)]
+    xs = [eye - n + f - g[:HALF] for n, f, g in zip(ns, seconds, both)]
+    cuts = [cut(g[HALF:]) for g in both]
+    both = [
+        product(cut(jnp.concatenate([x, g[HALF:]], axis=0)), y) for x, g, y in zip(xs, both, cuts)
+    ]
+    xs = [x + g[:HALF] for x, g in zip(xs, both)]
+    xs = [x + product(cut(x), cut(g[HALF:])) for x, g in zip(xs, both)]
+    bit = 4
     while (1 << bit) < HALF:
         inside = ((r >> (bit + 1)) == (c >> (bit + 1))) & ((r >> bit) != (c >> bit))
         cuts = [cut(x) for x in xs]
-        mids = []
-        for part, (xh, xl) in zip(lowers, cuts):
-            mh, ml = cut(jnp.where(inside, part, 0.0))
-            mids.append(dot(mh, xh) + (dot(mh, xl) + dot(ml, xh)))
-        news = []
-        for x, (xh, xl), mid in zip(xs, cuts, mids):
-            yh, yl = cut(mid)
-            news.append(x - (dot(xh, yh) + (dot(xh, yl) + dot(xl, yh))))
-        xs = news
+        mids = [product(cut(jnp.where(inside, part, 0.0)), x) for part, x in zip(lowers, cuts)]
+        xs = [x - product(y, cut(mid)) for x, y, mid in zip(xs, cuts, mids)]
         bit += 1
     for w in range(group):
         lower, scores, grown, left, final, right = data[w]
@@ -107,7 +121,8 @@
 
 def kernel(
     total, sections,
-    q_ref, k_ref, v_ref, ccol_ref, crow_ref, b_ref, gain_ref, out_ref, last_ref,
+    q_hbm, k_hbm, v_hbm, codes_ref, betas_ref, gain_ref, out_ref, last_ref,
+    q_ref, k_ref, v_ref, ccol_ref, crow_ref, b_ref, in_sem,
     ab, recv, o_ref, p_ref, sin, sout, ent, st, fin,
     map_send, map_recv, chain_send, chain_recv, ret_send, ret_recv, fin_send, fin_recv,
 ):
@@ -131,6 +146,12 @@
             barrier, inc=1, device_id={"sec": target}, device_id_type=pl.DeviceIdType.MESH
         )
 
+    copies = [
+        pltpu.make_async_copy(src, dst, in_sem.at[i])
+        for i, (src, dst) in enumerate(((q_hbm, q_ref), (k_hbm, k_ref), (v_hbm, v_ref)))
+    ]
+    for copy in copies:
+        copy.start()
     barrier = pltpu.get_barrier_semaphore()
     for i in range(1, plane):
         greet(base + (r + i) % plane)
@@ -140,6 +161,24 @@
     holders = planes - jnp.where(owner == place, 1, 0)
     expected = plane - 1 + jnp.where(at_end, holders, 1)
 
+    tokens = codes_ref.shape[0]
+    row = lax.broadcasted_iota(jnp.int32, (tokens, tokens), 0)
+    col = lax.broadcasted_iota(jnp.int32, (tokens, tokens), 1)
+    until = (row >= col).astype(F32).astype(BF16)
+    codes = codes_ref[...]
+    high = (codes >> 7).astype(F32).astype(BF16)
+    low = (codes & 127).astype(F32).astype(BF16)
+    cols = dot(until, high) * 128.0 + dot(until, low)
+    across = (((0,), (1,)), ((), ()))
+    crows = dot(high, until, across) * 128.0 + dot(low, until, across)
+    betas = betas_ref[...].astype(F32) * (1.0 / total)
+    for j in range(plane):
+        ccol_ref[j] = cols[:, j * kept : (j + 1) * kept]
+        crow_ref[j] = crows[j * kept : (j + 1) * kept]
+        b_ref[j] = betas[:, j * kept : (j + 1) * kept]
+    for copy in copies:
+        copy.wait()
+
     def send_map(h):
         return remote(ab.at[h], recv.at[r], map_send.at[h], map_recv.at[r], base + h)
 
@@ -256,19 +295,24 @@
     planes = sections // plane
     kept = heads // plane
     rows = heads * DK // sections
-    sums = jnp.cumsum(gate_codes, axis=0).astype(F32).reshape(tokens, plane, kept)
-    beta = (beta_codes.astype(F32) / total).reshape(tokens, plane, kept)
     vmem = pl.BlockSpec(memory_space=pltpu.VMEM)
     dma = pltpu.SemaphoreType.DMA
     return pl.pallas_call(
         functools.partial(kernel, total, sections),
-        in_specs=[vmem] * 7,
+        in_specs=[pl.BlockSpec(memory_space=pl.ANY)] * 3 + [vmem] * 3,
         out_specs=[vmem] * 2,
         out_shape=[
             jax.ShapeDtypeStruct((tokens, heads * DK), BF16),
             jax.ShapeDtypeStruct((rows, DK), F32),
         ],
         scratch_shapes=[
+            pltpu.VMEM(queries.shape, BF16),
+            pltpu.VMEM(keys.shape, BF16),
+            pltpu.VMEM(values.shape, BF16),
+            pltpu.VMEM((plane, tokens, kept), F32),
+            pltpu.VMEM((plane, kept, tokens), F32),
+            pltpu.VMEM((plane, tokens, kept), F32),
+            dma((3,)),
             pltpu.VMEM((plane, kept, DK, 2 * DK), F32),
             pltpu.VMEM((plane, kept, DK, 2 * DK), F32),
             pltpu.VMEM((plane, kept, tokens, DK), F32),
@@ -289,9 +333,8 @@
         queries,
         keys,
         values,
-        jnp.transpose(sums, (1, 0, 2)),
-        jnp.transpose(sums, (1, 2, 0)),
-        jnp.transpose(beta, (1, 0, 2)),
+        gate_codes,
+        beta_codes,
         norm_gain.reshape(1, DK),
     )
 

time: 72.8 us -> 70.2 us (0.964)
  Pallas kernels: 64.6 us -> 62.9 us
    pallas_call x1, Pallas kernels: 64.6 us -> 62.9 us  [shards(): pl.pallas_call(functools.partial(kernel, total, sections), in_specs=[pl.B...]
    unnamed x14, local copies, waits for them, and re-layouts: 5.55 us -> 6.37 us
where the time goes in v3:
time: 70.2 us; the launch traced here: 69.9 us
  Pallas kernels  62.9 us (90%)
  local copies, waits for them, and re-layouts  6.37 us (9%)
    pallas_call x1, Pallas kernels, shards(): pl.pallas_call(functools.partial(kernel, total, sections), in_specs=[pl.B...  62.9 us
    unnamed x14, local copies, waits for them, and re-layouts  6.37 us

profile of v3, /device:TPU:29, one launch (start us, length us, event | category | flops | bytes accessed | tf_op | source)
XLA Modules:
  0.0 69.9 jit_solution(4364083839104060287)
XLA Ops:
  0.6 0.0 copy-start.4
  0.6 0.8 %copy.8.codes_ref = s32[256,16]{1,0:T(8,128)S(1)} copy(s32[256,16]{0,1:T(8,128)} %param.9) | data formatting | bytes 32768 | tf_op args[3]
  1.5 0.0 copy-done.4
  1.5 0.0 copy-start.3
  1.5 0.1 copy.9.betas_ref
  1.6 0.5 copy-done.3
  2.1 0.0 copy-start
  2.1 1.2 %copy-done = bf16[256,2048]{1,0:T(8,128)(2,1)S(1)} copy-done((bf16[256,2048]{1,0:T(8,128)(2,1)S(1)}, bf16[256,2048]{1,0:T(8,128)(2,1)}, u32[]{:S(2)}) %copy-start) | copy-done | bytes 1048600
  3.4 0.0 copy-start.1
  3.4 1.0 %copy-done.1 = bf16[256,1024]{1,0:T(8,128)(2,1)S(1)} copy-done((bf16[256,1024]{1,0:T(8,128)(2,1)S(1)}, bf16[256,1024]{1,0:T(8,128)(2,1)}, u32[]{:S(2)}) %copy-start.1) | copy-done | bytes 524312
  4.4 0.0 copy-start.2
  4.4 1.0 %copy-done.2 = bf16[256,1024]{1,0:T(8,128)(2,1)S(1)} copy-done((bf16[256,1024]{1,0:T(8,128)(2,1)S(1)}, bf16[256,1024]{1,0:T(8,128)(2,1)}, u32[]{:S(2)}) %copy-start.2) | copy-done | bytes 524312
  5.4 62.9 %recurrence.1 = (bf16[256,2048]{1,0:T(8,128)(2,1)S(1)}, f32[64,128]{1,0:T(8,128)S(1)}) custom-call(bf16[256,1024]{1,0:T(8,128)(2,1)S(1)} %copy-done.1, bf16[256,1024]{1,0:T(8,128)(2,1)S(1)} %copy-done.2, bf16[256,2048]{1,0:T(8,128)(2,1)S(1)} %copy-done, s32[256,16]{1,0:T(8,128)S(1)} %copy.8.codes_ref, s32[256,16]{1,0:T(8,128)S(1)} %copy.9.betas_ref, ...), custom_call_target="tpu_custom_call" | custom-call | tf_op jit(solution)/shard_map/recurrence/pallas_call | solution.py:300
  68.3 1.0 %copy.12 = bf16[256,2048]{1,0:T(8,128)(2,1)} copy(bf16[256,2048]{1,0:T(8,128)(2,1)S(1)} %get-tuple-element.4) | data formatting | bytes 2097152
  69.3 0.6 copy.13
Async XLA Ops:
  0.6 0.8 %copy-start.4 = (s32[256,16]{0,1:T(8,128)S(1)}, s32[256,16]{0,1:T(8,128)}, u32[]{:S(2)}) copy-start(s32[256,16]{0,1:T(8,128)} %param.10) | copy-start | bytes 49156
  1.5 0.7 copy-start.3
  2.1 1.2 %copy-start = (bf16[256,2048]{1,0:T(8,128)(2,1)S(1)}, bf16[256,2048]{1,0:T(8,128)(2,1)}, u32[]{:S(2)}) copy-start(bf16[256,2048]{1,0:T(8,128)(2,1)} %v_hbm.1) | copy-start | bytes 3145732
  3.4 1.0 %copy-start.1 = (bf16[256,1024]{1,0:T(8,128)(2,1)S(1)}, bf16[256,1024]{1,0:T(8,128)(2,1)}, u32[]{:S(2)}) copy-start(bf16[256,1024]{1,0:T(8,128)(2,1)} %q_hbm.1) | copy-start | bytes 1572868
  4.4 1.0 %copy-start.2 = (bf16[256,1024]{1,0:T(8,128)(2,1)S(1)}, bf16[256,1024]{1,0:T(8,128)(2,1)}, u32[]{:S(2)}) copy-start(bf16[256,1024]{1,0:T(8,128)(2,1)} %k_hbm.1) | copy-start | bytes 1572868

commit v4 on v3

--- a/solution.py
+++ b/solution.py
@@ -41,21 +41,10 @@
     return product(cut(left), cut(right))
 
 
-def section_map(total, h, q_ref, k_ref, v_ref, ccol_ref, crow_ref, b_ref, ab_ref, o_ref, p_ref):
+def section_map(total, hs, q_ref, k_ref, v_ref, ccol_ref, crow_ref, b_ref, ab_ref, o_ref, p_ref):
     tokens = q_ref.shape[0]
     key_heads = q_ref.shape[1] // DK
     group = v_ref.shape[1] // DK // key_heads
-    q = q_ref[:, pl.ds(pl.multiple_of(h * DK, DK), DK)]
-    k = k_ref[:, pl.ds(pl.multiple_of(h * DK, DK), DK)]
-    v = v_ref[:, pl.ds(pl.multiple_of(h * group * DK, DK), group * DK)]
-    ccols, crows, betas = ccol_ref[h], crow_ref[h], b_ref[h]
-    qf = q.astype(F32)
-    kf = k.astype(F32)
-    rq = lax.rsqrt(jnp.sum(qf * qf, axis=1, keepdims=True) + 1e-06) * DK ** (-0.5)
-    rk = lax.rsqrt(jnp.sum(kf * kf, axis=1, keepdims=True) + 1e-06)
-    rk_row = jnp.transpose(jnp.broadcast_to(rk, (tokens, DK)))[0:1, :]
-    kk = dot(k, k, ROWS_BY_ROWS) * rk * rk_row
-    qk = dot(q, k, ROWS_BY_ROWS) * rq * rk_row
     row = lax.broadcasted_iota(jnp.int32, (tokens, tokens), 0)
     col = lax.broadcasted_iota(jnp.int32, (tokens, tokens), 1)
     r = row[:HALF, :HALF]
@@ -63,24 +52,36 @@
     eye = (r == c).astype(F32)
     blocks = tokens // HALF
     lowers, xs, data = [], [], []
-    for w in range(group):
-        ccol = ccols[:, w : w + 1]
-        crow = crows[w : w + 1, :]
-        beta = betas[:, w : w + 1]
-        gap = jnp.where(row >= col, (ccol - crow) * (-1.0 / total), -1e30)
-        mask = jnp.exp(gap)
-        lower = jnp.where(row > col, kk * mask * beta, 0.0)
-        grown = jnp.exp(ccol * (-1.0 / total))
-        last = ccol[tokens - 1 : tokens, :]
-        left = jnp.exp((last - ccol) * (-1.0 / total)) * rk
-        final = jnp.exp(last * (-1.0 / total))
-        right = jnp.concatenate(
-            [kf * (rk * beta * grown), v[:, w * DK : (w + 1) * DK].astype(F32) * beta], axis=1
-        )
-        data.append((lower, qk * mask, grown, left, final, right))
-        for b in range(blocks):
-            part = lower[b * HALF : (b + 1) * HALF, b * HALF : (b + 1) * HALF]
-            lowers.append(part)
+    for h in hs:
+        q = q_ref[:, pl.ds(pl.multiple_of(h * DK, DK), DK)]
+        k = k_ref[:, pl.ds(pl.multiple_of(h * DK, DK), DK)]
+        v = v_ref[:, pl.ds(pl.multiple_of(h * group * DK, DK), group * DK)]
+        ccols, crows, betas = ccol_ref[h], crow_ref[h], b_ref[h]
+        qf = q.astype(F32)
+        kf = k.astype(F32)
+        rq = lax.rsqrt(jnp.sum(qf * qf, axis=1, keepdims=True) + 1e-06) * DK ** (-0.5)
+        rk = lax.rsqrt(jnp.sum(kf * kf, axis=1, keepdims=True) + 1e-06)
+        rk_row = jnp.transpose(jnp.broadcast_to(rk, (tokens, DK)))[0:1, :]
+        kk = dot(k, k, ROWS_BY_ROWS) * rk * rk_row
+        qk = dot(q, k, ROWS_BY_ROWS) * rq * rk_row
+        for w in range(group):
+            ccol = ccols[:, w : w + 1]
+            crow = crows[w : w + 1, :]
+            beta = betas[:, w : w + 1]
+            gap = jnp.where(row >= col, (ccol - crow) * (-1.0 / total), -1e30)
+            mask = jnp.exp(gap)
+            lower = jnp.where(row > col, kk * mask * beta, 0.0)
+            grown = jnp.exp(ccol * (-1.0 / total))
+            last = ccol[tokens - 1 : tokens, :]
+            left = jnp.exp((last - ccol) * (-1.0 / total)) * rk
+            final = jnp.exp(last * (-1.0 / total))
+            right = jnp.concatenate(
+                [kf * (rk * beta * grown), v[:, w * DK : (w + 1) * DK].astype(F32) * beta], axis=1
+            )
+            data.append((h, w, k, qf * (rq * grown), lower, qk * mask, left, final, right))
+            for b in range(blocks):
+                part = lower[b * HALF : (b + 1) * HALF, b * HALF : (b + 1) * HALF]
+                lowers.append(part)
     near = (r >> 4) == (c >> 4)
     ns = [jnp.where(near, part, 0.0) for part in lowers]
     seconds = [product(x, x) for x in map(cut, ns)]
@@ -100,19 +101,18 @@
         mids = [product(cut(jnp.where(inside, part, 0.0)), x) for part, x in zip(lowers, cuts)]
         xs = [x - product(y, cut(mid)) for x, y, mid in zip(xs, cuts, mids)]
         bit += 1
-    for w in range(group):
-        lower, scores, grown, left, final, right = data[w]
+    for n, (h, w, k, reach, lower, scores, left, final, right) in enumerate(data):
         parts = []
         for b in range(blocks):
             rows = slice(b * HALF, (b + 1) * HALF)
             rhs = right[rows]
             for e in range(b):
                 rhs = rhs - dot3(lower[rows, e * HALF : (e + 1) * HALF], parts[e])
-            parts.append(dot3(xs[w * blocks + b], rhs))
+            parts.append(dot3(xs[n * blocks + b], rhs))
         solved = jnp.concatenate(parts, axis=0)
         read = dot3(scores, solved)
         o_ref[h, w] = read[:, DK:]
-        p_ref[h, w] = qf * (rq * grown) - read[:, :DK]
+        p_ref[h, w] = reach - read[:, :DK]
         sh, sl = cut(solved * left)
         moved = dot(k, sh, DOWN) + dot(k, sl, DOWN)
         ab_ref[h, w, :, :DK] = final * eye - moved[:, :DK]
@@ -182,14 +182,17 @@
     def send_map(h):
         return remote(ab.at[h], recv.at[r], map_send.at[h], map_recv.at[r], base + h)
 
-    def one_head(i, carry):
-        h = (r + 1 + i) % plane
-        section_map(total, h, q_ref, k_ref, v_ref, ccol_ref, crow_ref, b_ref, ab, o_ref, p_ref)
+    def two_heads(i, carry):
+        one, two = (r + 1 + 2 * i) % plane, (r + 2 + 2 * i) % plane
+        section_map(
+            total, (one, two), q_ref, k_ref, v_ref, ccol_ref, crow_ref, b_ref, ab, o_ref, p_ref
+        )
         pl.when(i == 0)(lambda: pl.semaphore_wait(barrier, expected))
-        pl.when(i < plane - 1)(lambda: send_map(h).start())
+        send_map(one).start()
+        pl.when(i < plane // 2 - 1)(lambda: send_map(two).start())
         return carry
 
-    lax.fori_loop(0, plane, one_head, 0)
+    lax.fori_loop(0, plane // 2, two_heads, 0)
     recv[r] = ab[r]
 
     for s in range(plane):
@@ -299,7 +302,7 @@
     dma = pltpu.SemaphoreType.DMA
     return pl.pallas_call(
         functools.partial(kernel, total, sections),
-        in_specs=[pl.BlockSpec(memory_space=pl.ANY)] * 3 + [vmem] * 3,
+        in_specs=[pl.BlockSpec(memory_space=pltpu.HBM)] * 3 + [vmem] * 3,
         out_specs=[vmem] * 2,
         out_shape=[
             jax.ShapeDtypeStruct((tokens, heads * DK), BF16),

time: 70.2 us -> 67.3 us (0.959)
  Pallas kernels: 62.9 us -> 59.9 us
    pallas_call x1, Pallas kernels: 62.9 us -> 59.9 us  [shards(): pl.pallas_call(functools.partial(kernel, total, sections), in_specs=[pl.B...]
where the time goes in v4:
time: 67.3 us; the launch traced here: 67 us
  Pallas kernels  59.9 us (89%)
  local copies, waits for them, and re-layouts  6.37 us (9%)
    pallas_call x1, Pallas kernels, shards(): pl.pallas_call(functools.partial(kernel, total, sections), in_specs=[pl.B...  59.9 us
    unnamed x14, local copies, waits for them, and re-layouts  6.37 us

profile of v4, /device:TPU:29, one launch (start us, length us, event | category | flops | bytes accessed | tf_op | source)
XLA Modules:
  0.0 67.0 jit_solution(14664721923300411973)
XLA Ops:
  0.6 0.0 copy-start.4
  0.6 0.8 %copy.8.codes_ref = s32[256,16]{1,0:T(8,128)S(1)} copy(s32[256,16]{0,1:T(8,128)} %param.9) | data formatting | bytes 32768 | tf_op args[3]
  1.5 0.0 copy-done.4
  1.5 0.0 copy-start.3
  1.5 0.1 copy.9.betas_ref
  1.6 0.5 copy-done.3
  2.1 0.0 copy-start
  2.1 1.2 %copy-done = bf16[256,2048]{1,0:T(8,128)(2,1)S(1)} copy-done((bf16[256,2048]{1,0:T(8,128)(2,1)S(1)}, bf16[256,2048]{1,0:T(8,128)(2,1)}, u32[]{:S(2)}) %copy-start) | copy-done | bytes 1048600
  3.4 0.0 copy-start.1
  3.4 1.0 %copy-done.1 = bf16[256,1024]{1,0:T(8,128)(2,1)S(1)} copy-done((bf16[256,1024]{1,0:T(8,128)(2,1)S(1)}, bf16[256,1024]{1,0:T(8,128)(2,1)}, u32[]{:S(2)}) %copy-start.1) | copy-done | bytes 524312
  4.4 0.0 copy-start.2
  4.4 1.0 %copy-done.2 = bf16[256,1024]{1,0:T(8,128)(2,1)S(1)} copy-done((bf16[256,1024]{1,0:T(8,128)(2,1)S(1)}, bf16[256,1024]{1,0:T(8,128)(2,1)}, u32[]{:S(2)}) %copy-start.2) | copy-done | bytes 524312
  5.4 59.9 %recurrence.1 = (bf16[256,2048]{1,0:T(8,128)(2,1)S(1)}, f32[64,128]{1,0:T(8,128)S(1)}) custom-call(bf16[256,1024]{1,0:T(8,128)(2,1)S(1)} %copy-done.1, bf16[256,1024]{1,0:T(8,128)(2,1)S(1)} %copy-done.2, bf16[256,2048]{1,0:T(8,128)(2,1)S(1)} %copy-done, s32[256,16]{1,0:T(8,128)S(1)} %copy.8.codes_ref, s32[256,16]{1,0:T(8,128)S(1)} %copy.9.betas_ref, ...), custom_call_target="tpu_custom_call" | custom-call | tf_op jit(solution)/shard_map/recurrence/pallas_call | solution.py:303
  65.4 1.0 %copy.12 = bf16[256,2048]{1,0:T(8,128)(2,1)} copy(bf16[256,2048]{1,0:T(8,128)(2,1)S(1)} %get-tuple-element.4) | data formatting | bytes 2097152
  66.4 0.6 copy.13
Async XLA Ops:
  0.6 0.8 %copy-start.4 = (s32[256,16]{0,1:T(8,128)S(1)}, s32[256,16]{0,1:T(8,128)}, u32[]{:S(2)}) copy-start(s32[256,16]{0,1:T(8,128)} %param.10) | copy-start | bytes 49156
  1.5 0.7 copy-start.3
  2.1 1.2 %copy-start = (bf16[256,2048]{1,0:T(8,128)(2,1)S(1)}, bf16[256,2048]{1,0:T(8,128)(2,1)}, u32[]{:S(2)}) copy-start(bf16[256,2048]{1,0:T(8,128)(2,1)} %v_hbm.1) | copy-start | bytes 3145732
  3.4 1.0 %copy-start.1 = (bf16[256,1024]{1,0:T(8,128)(2,1)S(1)}, bf16[256,1024]{1,0:T(8,128)(2,1)}, u32[]{:S(2)}) copy-start(bf16[256,1024]{1,0:T(8,128)(2,1)} %q_hbm.1) | copy-start | bytes 1572868
  4.4 1.0 %copy-start.2 = (bf16[256,1024]{1,0:T(8,128)(2,1)S(1)}, bf16[256,1024]{1,0:T(8,128)(2,1)}, u32[]{:S(2)}) copy-start(bf16[256,1024]{1,0:T(8,128)(2,1)} %k_hbm.1) | copy-start | bytes 1572868
